TPU v7x, 256 devices: a whole 4x4x8 slice. The times are simulated.
256 devices in a mesh: ia: 32 (over z, x), ja: 4 (over y), ka: 2 (over core).
Axes of the slice: x: 4, y: 4, z: 8, core: 2. Of those that a mesh axis runs over, the one named last changes fastest.
Arguments:
- tensor: bfloat16 [4, 16384, 16384], P('ka', 'ia', 'ja'), may hold values from -6144 to 6144
- factor_b: bfloat16 [4, 4096, 256], P('ja', ('ia', 'ka')), may hold values from -180 to 180
- factor_c: bfloat16 [2, 2, 256], P('ka'), may hold values from 0.5 to 1.5
Outputs:
- factor_a: float32 [32, 512, 256], P('ia', ('ja', 'ka'))
All inputs are finite; a program needn't handle non-finite values.
Results may differ from a plain program's by a relative error of at most 0.0003.
Values may be sent and summed in bfloat16 or wider, within the bound.
A program may use at most 64 MiB of HBM per device.

v0:
```python
import jax
import jax.numpy as jnp
from jax import lax
from jax.sharding import PartitionSpec as P


def solve_rows(lower, rows):
    middle = lax.linalg.triangular_solve(lower, rows, left_side=False, lower=True, transpose_a=True)
    return lax.linalg.triangular_solve(
        lower, middle, left_side=False, lower=True, transpose_a=False
    )


def per_device(tensor, factor_b, factor_c):
    rank = factor_b.shape[2]
    c_rows = factor_c[0].astype(jnp.float32)
    gram_block = jnp.zeros((rank, rank), jnp.float32)
    totals = jnp.einsum(
        "kin,nr->kir",
        tensor,
        lax.all_gather(factor_b, ("ia", "ka"), axis=1, tiled=True)[0],
        preferred_element_type=jnp.float32,
    )
    per_slab, gram_block = (totals, gram_block)
    mttkrp = jnp.sum(per_slab * c_rows[:, None, :], axis=0)
    local_c = jnp.dot(factor_c[0].T, factor_c[0], preferred_element_type=jnp.float32)
    own_rows = factor_b[0]
    gram_own = jnp.dot(own_rows.T, own_rows, preferred_element_type=jnp.float32)
    gram_b = lax.psum(gram_own, ("ia", "ja", "ka"))
    gram_c = lax.psum(local_c, "ka")
    lower = jnp.linalg.cholesky(gram_b * gram_c)
    shares = solve_rows(
        lower, lax.psum_scatter(mttkrp, ("ja", "ka"), scatter_dimension=0, tiled=True)
    )
    return shares[None]


def solution(mesh):
    return jax.shard_map(
        per_device,
        mesh=mesh,
        in_specs=(P("ka", "ia", "ja"), P("ja", ("ia", "ka"), None), P("ka", None, None)),
        out_specs=P("ia", ("ja", "ka"), None),
        check_vma=False,
    )
```

profile of v0, /device:TPU:1, one launch (start us, length us, event | category | flops | bytes accessed | tf_op | source)
XLA Modules:
  0.0 384.8 jit_solution(9537300040272275014)
XLA Ops:
  7.4 1.8 fusion.19
  9.2 1.7 fusion.21
  10.9 0.0 all-gather.2.cloned.1.call-start
  11.0 0.5 all-gather.2.cloned.1.call-update
  11.6 0.7 bitcast_convert_fusion
  12.3 254.9 %all-reduce.4.cloned.1.call-done = f32[256,256]{0,1:T(8,128)} async-done(((f32[256,256]{0,1:T(8,128)}), f32[256,256]{0,1:T(8,128)}) %all-reduce.4.cloned.1.call-update) | async-done | bytes 262160 | tf_op jit(solution)/shard_map/psum | solution.py:29
  267.1 32.5 %all-reduce.6.cloned.1.call-done = f32[256,256]{0,1:T(8,128)} async-done(((f32[256,256]{0,1:T(8,128)}), f32[256,256]{0,1:T(8,128)}) %all-reduce.6.cloned.1.call-update) | async-done | bytes 262160 | tf_op jit(solution)/shard_map/psum | solution.py:30
  299.6 1.1 mul.13
  300.7 0.1 copy.6
  300.8 0.1 fusion.8
  300.9 11.7 %cholesky.50 = f32[128,128]{1,0:T(8,128)S(1)} custom-call(f32[128,128]{1,0:T(8,128)S(1)} %cholesky.118), custom_call_target="Cholesky" | custom-call | tf_op jit(solution)/shard_map/jit(cholesky)/cholesky | solution.py:31
  312.6 9.8 %custom-call.16 = f32[1,128,128]{1,2,0:T(8,128)S(1)} custom-call(f32[1,128,128]{2,1,0:T(8,128)S(1)} %get-tuple-element.26), custom_call_target="InvertDiagBlocksLowerTriangular" | custom-call | tf_op jit(solution)/shard_map/jit(cholesky)/cholesky | solution.py:31
  322.5 0.2 constant_dynamic-update-slice_fusion.1
  322.7 0.3 convolution_subtract_fusion
  322.9 11.7 %cholesky.105 = f32[128,128]{1,0:T(8,128)S(1)} custom-call(f32[128,128]{1,0:T(8,128)S(1)} %convolution_subtract_fusion), custom_call_target="Cholesky" | custom-call | tf_op jit(solution)/shard_map/jit(cholesky)/cholesky | solution.py:31
  334.7 7.3 %fusion.5 = f32[512,256]{1,0:T(8,128)} fusion(bf16[2,512,4096]{2,1,0:T(8,128)(2,1)} %param.3, bf16[1,4096,256]{2,1,0:T(8,128)(2,1)} %all-gather.2.cloned.1.call-done, f32[2,256]{1,0:T(2,128)S(1)} %bitcast_convert_fusion), kind=kOutput, calls=%fused_computation.5 | convolution fusion | flops 2147876864 | bytes 11012096 | tf_op jit(solution)/shard_map/kin,nr->kir/dot_general | solution.py:18
  342.1 0.7 compare_reduce_fusion
  344.0 0.1 triangular_solve.67
  344.1 3.9 %while.1 = (s32[]{:T(128)}, f32[256,256]{1,0:T(8,128)S(1)}, s32[2,2]{1,0:T(2,128)S(1)}, f32[2,128,128]{2,1,0:T(8,128)S(1)}, s32[]{:T(128)}) while((s32[]{:T(128)}, f32[256,256]{1,0:T(8,128)S(1)}, s32[2,2]{1,0:T(2,128)S(1)}, f32[2,128,128]{2,1,0:T(8,128)S(1)}, s32[]{:T(128)}) %tuple.23), condition=%wide.while_cond, body=%wide.while_body.sunk | while | flops 2 | bytes 131189 | solution.py:8
  344.1 0.6 fusion.33
  344.7 1.3 bitcast_dynamic-update-slice_fusion.2
  346.1 0.6 fusion.33
  346.7 1.3 bitcast_dynamic-update-slice_fusion.2
  348.0 19.7 %custom-call.17 = f32[2,128,128]{1,2,0:T(8,128)S(1)} custom-call(f32[2,128,128]{2,1,0:T(8,128)S(1)} %get-tuple-element.12), custom_call_target="InvertDiagBlocksLowerTriangular" | custom-call | tf_op jit(solution)/shard_map/triangular_solve | solution.py:8
  367.7 6.3 %reduce-scatter.2.cloned.1.call-done = f32[64,256]{1,0:T(8,128)} async-done(((f32[512,256]{1,0:T(8,128)}), f32[64,256]{1,0:T(8,128)}) %reduce-scatter.2.cloned.1.call-update) | async-done | bytes 65552 | tf_op jit(solution)/shard_map/reduce_scatter | solution.py:33
  373.9 0.9 fusion.13
  374.9 1.0 convolution_subtract_fusion.2
  375.9 0.2 fusion.15
  376.1 0.2 fusion.14
  376.3 0.2 convolution_subtract_fusion.1
  376.5 0.2 fusion.12
  376.8 0.6 maximum_bitcast_fusion
  (16 shorter events, 0.3 us)
Async XLA Ops:
  7.4 259.8 %all-reduce.4.cloned.1.call-start = ((), (), s32[]{:S(2)}) async-start(), calls=%async_computation.3 | async-start | bytes 524288 | tf_op jit(solution)/shard_map/psum | solution.py:29
  9.2 290.5 %all-reduce.6.cloned.1.call-start = ((), (), s32[]{:S(2)}) async-start(), calls=%async_computation.4 | async-start | bytes 524288 | tf_op jit(solution)/shard_map/psum | solution.py:30
  10.9 323.8 %all-gather.2.cloned.1.call-start = ((), (), s32[]{:S(2)}) async-start(), calls=%async_computation.1 | async-start | bytes 2129920 | tf_op jit(solution)/shard_map/all_gather | solution.py:21
  11.5 362.4 %reduce-scatter.2.cloned.1.call-start = ((), (), s32[]{:S(2)}) async-start(), calls=%async_computation.2 | async-start | bytes 589824 | tf_op jit(solution)/shard_map/reduce_scatter | solution.py:33
Sparse Core Ops, SparseCore 0:
  13.6 253.4 all-reduce.3
  269.7 29.8 all-reduce.5
Sparse Core Ops, SparseCore 1:
  14.5 81.7 all-gather.1
  342.1 31.8 reduce-scatter.1
where the time goes:
time: 387 us; the launch traced here: 385 us
  waiting for transfers between devices  294 us (76%)
  other arithmetic  56.1 us (14%)
  between operations  16.2 us (4%)
  matrix products  14 us (4%)
  local copies, waits for them, and re-layouts  4.1 us (1%)
    psum x1, waiting for transfers between devices, per_device(): gram_b = lax.psum(gram_own, ('ia', 'ja', 'ka'))  255 us
    another operation x6, other arithmetic, per_device(): lower = jnp.linalg.cholesky(gram_b * gram_c)  34 us
    psum x1, waiting for transfers between devices, per_device(): gram_c = lax.psum(local_c, 'ka')  32.5 us
    another operation x3, other arithmetic, solve_rows(): lax.linalg.triangular_solve(lower, rows, left_side=False, lower=True, tra...  19.7 us
  transfers between devices with their start and end apart: 4, of which 3 were waited for; matrix products, arithmetic and copies ran while one was open for 16% of the time, Pallas kernels for 0%

commit v1 on v0

v1 whole, which is shorter than its diff:
```python
import jax, jax.numpy as jnp
from jax import lax
from jax.experimental import pallas as pl
from jax.sharding import PartitionSpec as P
HI=lax.Precision.HIGHEST


def dot(a,b,ta=False,tb=False):
    return lax.dot_general(a,b,(((0 if ta else 1,),(1 if tb else 0,)),((),())),precision=HI,preferred_element_type=jnp.float32)


def gj128(block):
    tiles=[block[8*q:8*q+8,:] for q in range(16)]
    lane=lax.broadcasted_iota(jnp.int32,(8,128),1)
    sub=lax.broadcasted_iota(jnp.int32,(8,128),0)
    lb=lambda v,k: jnp.broadcast_to(v[:,k:k+1],(8,128))
    sb=lambda v,i: jnp.broadcast_to(v[i:i+1,:],(8,128))
    for p in range(16):
        cols=[lb(tiles[p],8*p+m) for m in range(8)]
        for s in range(4):
            i0,i1=2*s,2*s+1
            k0,k1=8*p+i0,8*p+i1
            c0,c1=cols[i0],cols[i1]
            a,b,d=sb(c0,i0),sb(c1,i0),sb(c1,i1)
            r=1.0/(a*d-b*b)
            at0,at1=lane==k0,lane==k1
            either=at0|at1
            rows=(sub==i0)|(sub==i1)
            e0=jnp.where(sub==i0,-1.0,jnp.where(sub==i1,0.0,c0))
            e1=jnp.where(sub==i1,-1.0,jnp.where(sub==i0,0.0,c1))
            T=tiles[p]
            row0,row1=sb(T,i0),sb(T,i1)
            w0=jnp.where(at0,-d,jnp.where(at1,b,d*row0-b*row1))*r
            w1=jnp.where(at0,b,jnp.where(at1,-a,a*row1-b*row0))*r
            for m in range(i1+1,8):
                t0,t1=sb(cols[m],i0),sb(cols[m],i1)
                g=e0*(d*t0-b*t1)+e1*(a*t1-b*t0)
                cols[m]=jnp.where(rows,0.0,cols[m])-g*r
            new=[]
            for q in range(16):
                t=tiles[q]
                if q==p:
                    new.append(jnp.where(either|rows,0.0,t)-e0*w0-e1*w1)
                else:
                    new.append(jnp.where(either,0.0,t)-lb(t,k0)*w0-lb(t,k1)*w1)
            tiles=new
    return -jnp.concatenate(tiles,axis=0)


def solve_kernel(gb_ref,c_ref,m_ref,o_ref):
    c=c_ref[...]
    gc=lax.dot_general(c,c,(((0,),(0,)),((),())),preferred_element_type=jnp.float32)
    n=gb_ref[...]*gc
    eye=lax.broadcasted_iota(jnp.int32,n.shape,0)==lax.broadcasted_iota(jnp.int32,n.shape,1)
    diag=jnp.where(eye,n,0.0)
    sr=lax.rsqrt(jnp.sum(diag,axis=0,keepdims=True))
    sc=lax.rsqrt(jnp.sum(diag,axis=1,keepdims=True))
    n=n*sr*sc
    m=m_ref[...]*sr
    n11,n12,n22=n[:128,:128],n[:128,128:],n[128:,128:]
    m1,m2=m[:,:128],m[:,128:]
    i1=gj128(n11)
    t=dot(i1,n12)
    i2=gj128(n22-dot(n12,t,ta=True))
    z=dot(m2-dot(m1,t),i2)
    a1=dot(m1,i1)-dot(z,t,tb=True)
    o_ref[...]=jnp.concatenate([a1,z],axis=1)*sr


def per_device(tensor, factor_b, factor_c):
    block = lax.all_gather(factor_b, ("ia", "ka"), axis=1, tiled=True)[0]
    gram = lax.dot_general(
        block, block, (((0,), (0,)), ((), ())), preferred_element_type=jnp.float32
    )
    gram = lax.psum(gram, "ja")
    c_all = lax.all_gather(factor_c[0], "ka", axis=0, tiled=True)
    slabs = jnp.einsum("kin,nr->kir", tensor, block, preferred_element_type=jnp.float32)
    mttkrp = jnp.sum(slabs * factor_c[0].astype(jnp.float32)[:, None, :], axis=0)
    rows = lax.psum_scatter(mttkrp, ("ja", "ka"), scatter_dimension=0, tiled=True)
    out = pl.pallas_call(
        solve_kernel, out_shape=jax.ShapeDtypeStruct(rows.shape, jnp.float32), name="solve"
    )(gram, c_all, rows)
    return out[None]


def solution(mesh):
    return jax.shard_map(
        per_device,
        mesh=mesh,
        in_specs=(P("ka", "ia", "ja"), P("ja", ("ia", "ka"), None), P("ka", None, None)),
        out_specs=P("ia", ("ja", "ka"), None),
        check_vma=False,
    )
```

time: 387 us -> 198 us (0.51)
  waiting for transfers between devices: 294 us -> 154 us
  other arithmetic: 56.1 us -> 0.68 us
  Pallas kernels: 0 us -> 15.4 us
    psum x2 -> x1, waiting for transfers between devices: 287 us -> 33.1 us  [per_device(): gram = lax.psum(gram, 'ja')]
    all_gather x1, waiting for transfers between devices: 0.03 us -> 83.6 us  [per_device(): block = lax.all_gather(factor_b, ('ia', 'ka'), axis=1, tiled=True)[0]]
    another operation x9 -> x0, other arithmetic: 53.7 us -> none  [the longest x6 34 us: per_device(): lower = jnp.linalg.cholesky(gram_b * gram_c)]
    reduce_scatter x1, waiting for transfers between devices: 6.26 us -> 36.5 us  [per_device(): lax.psum_scatter(mttkrp, ('ja', 'ka'), scatter_dimension=0, tiled=True)]
    pallas_call x0 -> x1, Pallas kernels: none -> 15.4 us  [per_device(): pl.pallas_call(solve_kernel, out_shape=jax.ShapeDtypeStruct(rows.shape, j...]
    another operation x9 -> x0, local copies, waits for them, and re-layouts: 3.97 us -> none
    dot_general x3 -> x2, matrix products: 10.8 us -> 10.4 us  [the longest x1 6.56 us: per_device(): jnp.einsum('kin,nr->kir', tensor, block, preferred_element_type=jnp.float32)]
  transfers between devices with their start and end apart: 4 -> 3, of which waited for: 3 -> 3; matrix products, arithmetic and copies ran while one was open for 16% -> 4% of each run, Pallas kernels for 0% -> 0%
where the time goes in v1:
time: 198 us; the launch traced here: 196 us
  waiting for transfers between devices  154 us (78%)
  Pallas kernels  15.4 us (8%)
  between operations  13.1 us (7%)
  matrix products  10.4 us (5%)
    all_gather x1, waiting for transfers between devices, per_device(): block = lax.all_gather(factor_b, ('ia', 'ka'), axis=1, tiled=True)[0]  83.6 us
    reduce_scatter x1, waiting for transfers between devices, per_device(): lax.psum_scatter(mttkrp, ('ja', 'ka'), scatter_dimension=0, tiled=True)  36.5 us
    psum x1, waiting for transfers between devices, per_device(): gram = lax.psum(gram, 'ja')  33.1 us
    pallas_call x1, Pallas kernels, per_device(): pl.pallas_call(solve_kernel, out_shape=jax.ShapeDtypeStruct(rows.shape, j...  15.4 us
    dot_general x1, matrix products, per_device(): jnp.einsum('kin,nr->kir', tensor, block, preferred_element_type=jnp.float32)  6.56 us
  transfers between devices with their start and end apart: 3, of which 3 were waited for; matrix products, arithmetic and copies ran while one was open for 4% of the time, Pallas kernels for 0%

profile of v1, /device:TPU:1, one launch (start us, length us, event | category | flops | bytes accessed | tf_op | source)
XLA Modules:
  0.0 196.0 jit_solution(4135701912208298328)
XLA Ops:
  6.5 0.0 all-gather.3.cloned.1.call-start
  6.5 0.7 all-gather.3.cloned.1.call-update
  7.3 0.0 all-reduce.2.cloned.1.call-start
  7.3 0.7 bitcast_convert_fusion
  8.0 83.6 %all-gather.3.cloned.1.call-done = bf16[1,4096,256]{2,1,0:T(8,128)(2,1)} async-done(((bf16[1,64,256]{2,1,0:T(8,128)(2,1)}), bf16[1,4096,256]{2,1,0:T(8,128)(2,1)}) %all-gather.3.cloned.1.call-update) | async-done | bytes 2097168 | tf_op jit(solution)/shard_map/all_gather | solution.py:71
  91.6 0.0 copy-start.1
  91.6 3.8 %fusion.2 = f32[256,256]{1,0:T(8,128)} fusion(bf16[1,4096,256]{2,1,0:T(8,128)(2,1)} %all-gather.3.cloned.1.call-done), kind=kOutput, calls=%fused_computation.2 | convolution fusion | flops 536870912 | bytes 2359296 | tf_op jit(solution)/shard_map/dot_general | solution.py:72
  95.4 0.0 all-reduce.2.cloned.1.call-update
  95.4 0.0 copy-start
  95.4 0.0 reduce-scatter.2.cloned.1.call-start
  95.5 0.0 copy-done.1
  95.5 6.6 %fusion.7 = f32[512,256]{1,0:T(8,128)} fusion(bf16[2,512,4096]{2,1,0:T(8,128)(2,1)} %param.3, bf16[1,4096,256]{2,1,0:T(8,128)(2,1)S(1)} %copy-done.1, f32[2,256]{1,0:T(2,128)S(1)} %bitcast_convert_fusion), kind=kOutput, calls=%fused_computation.5 | convolution fusion | flops 2147876864 | bytes 11012096 | tf_op jit(solution)/shard_map/kin,nr->kir/dot_general | solution.py:77
  102.0 0.0 reduce-scatter.2.cloned.1.call-update
  102.1 0.0 copy-done
  102.1 1.8 all-gather
  103.9 0.6 copy.8
  104.5 33.1 %all-reduce.2.cloned.1.call-done.gb_ref = f32[256,256]{1,0:T(8,128)} async-done(((f32[256,256]{1,0:T(8,128)}), f32[256,256]{1,0:T(8,128)}) %all-reduce.2.cloned.1.call-update) | async-done | bytes 262160 | tf_op jit(solution)/shard_map/psum | solution.py:75
  137.6 36.5 %reduce-scatter.2.cloned.1.call-done.m_ref = f32[64,256]{1,0:T(8,128)} async-done(((f32[512,256]{1,0:T(8,128)}), f32[64,256]{1,0:T(8,128)}) %reduce-scatter.2.cloned.1.call-update) | async-done | bytes 65552 | tf_op jit(solution)/shard_map/reduce_scatter | solution.py:79
  174.1 15.4 %solve.1 = f32[64,256]{1,0:T(8,128)} custom-call(f32[256,256]{1,0:T(8,128)} %all-reduce.2.cloned.1.call-done.gb_ref, bf16[4,256]{1,0:T(4,128)(2,1)} %bitcast.18, f32[64,256]{1,0:T(8,128)} %reduce-scatter.2.cloned.1.call-done.m_ref), custom_call_target="tpu_custom_call" | custom-call | tf_op jit(solution)/shard_map/solve/pallas_call | solution.py:80
  (1 shorter events, 0.0 us)
Async XLA Ops:
  6.5 85.0 %all-gather.3.cloned.1.call-start = ((), (), s32[]{:S(2)}) async-start(), calls=%async_computation.1 | async-start | bytes 2129920 | tf_op jit(solution)/shard_map/all_gather | solution.py:71
  7.3 130.3 %all-reduce.2.cloned.1.call-start = ((), (), s32[]{:S(2)}) async-start(), calls=%async_computation.2 | async-start | bytes 524288 | tf_op jit(solution)/shard_map/psum | solution.py:75
  91.6 3.9 %copy-start.1 = (bf16[1,4096,256]{2,1,0:T(8,128)(2,1)S(1)}, bf16[1,4096,256]{2,1,0:T(8,128)(2,1)}, u32[]{:S(2)}) copy-start(bf16[1,4096,256]{2,1,0:T(8,128)(2,1)} %all-gather.3.cloned.1.call-done) | copy-start | bytes 6291460
  95.4 6.7 %copy-start = (bf16[1,2,256]{2,1,0:T(2,128)(2,1)S(1)}, bf16[1,2,256]{2,1,0:T(2,128)(2,1)}, u32[]{:S(2)}) copy-start(bf16[1,2,256]{2,1,0:T(2,128)(2,1)} %param.5) | copy-start | bytes 3076
  95.4 78.6 %reduce-scatter.2.cloned.1.call-start = ((), (), s32[]{:S(2)}) async-start(), calls=%async_computation.3 | async-start | bytes 589824 | tf_op jit(solution)/shard_map/reduce_scatter | solution.py:79
Sparse Core Ops, SparseCore 0:
  10.1 81.3 all-gather.2
  95.5 41.9 all-reduce.1
  140.2 33.7 reduce-scatter.1

commit v2 on v1

--- a/solution.py
+++ b/solution.py
@@ -1,6 +1,7 @@
 import jax, jax.numpy as jnp
 from jax import lax
 from jax.experimental import pallas as pl
+from jax.experimental.pallas import tpu as pltpu
 from jax.sharding import PartitionSpec as P
 HI=lax.Precision.HIGHEST
 
@@ -48,7 +49,7 @@
 
 
 def solve_kernel(gb_ref,c_ref,m_ref,o_ref):
-    c=c_ref[...]
+    c=c_ref[...].astype(jnp.bfloat16)
     gc=lax.dot_general(c,c,(((0,),(0,)),((),())),preferred_element_type=jnp.float32)
     n=gb_ref[...]*gc
     eye=lax.broadcasted_iota(jnp.int32,n.shape,0)==lax.broadcasted_iota(jnp.int32,n.shape,1)
@@ -67,18 +68,210 @@
     o_ref[...]=jnp.concatenate([a1,z],axis=1)*sr
 
 
+Z, X, Y, CORES = 8, 4, 4, 2
+PIECE = 64
+RANK = 256
+MESH = pl.DeviceIdType.MESH
+
+
+def distance(step):
+    return lax.rem(step, 2) * ((step + 1) // 2) + (1 - lax.rem(step, 2)) * lax.rem(Z - step // 2, Z)
+
+
+def gather_kernel(
+    x_hbm, b_ref, c_ref,
+    gram_out, c_out, m_out,
+    xbuf, bbuf, acc, gacc, grecv, gsum, gall, cbuf, comb, ccore, csum, crecv_y,
+    x_sem, z_send, z_recv, g_send, g_recv, k_send, k_recv, c_send, c_recv,
+    gs_send, gs_recv, ga_send, ga_recv, mc_send, mc_recv, my_send, my_recv,
+):
+    ia, y, c = lax.axis_index("ia"), lax.axis_index("ja"), lax.axis_index("ka")
+    z, x = ia // X, lax.rem(ia, X)
+    peer = (ia, y, 1 - c)
+
+    def at(dz=0, dx=0, dy=0, core=None):
+        zz, xx = lax.rem(z + dz, Z), lax.rem(x + dx, X)
+        return (zz * X + xx, lax.rem(y + dy, Y), c if core is None else core)
+
+    def send(src, dst, ss, rs, to):
+        copy = pltpu.make_async_remote_copy(
+            src_ref=src, dst_ref=dst, send_sem=ss, recv_sem=rs, device_id=to, device_id_type=MESH
+        )
+        copy.start()
+
+    def arrived(ref, sem):
+        pltpu.make_async_remote_copy(
+            src_ref=ref, dst_ref=ref, send_sem=sem, recv_sem=sem, device_id=peer, device_id_type=MESH
+        ).wait_recv()
+
+    def load(step):
+        zz = lax.rem(z + distance(step), Z)
+        return pltpu.make_async_copy(
+            x_hbm.at[:, :, pl.ds(pl.multiple_of(zz * 512, 512), 512)], xbuf.at[zz], x_sem.at[step]
+        )
+
+    partners = [at(dz=d) for d in range(1, Z)] + [at(dx=d) for d in range(1, X)]
+    partners += [at(dy=d) for d in range(1, Y)] + [at(dy=d, core=1 - c) for d in range(1, Y)] + [peer]
+    barrier = pltpu.get_barrier_semaphore()
+    for to in partners:
+        pl.semaphore_signal(barrier, inc=1, device_id=to, device_id_type=MESH)
+    for step in range(Z):
+        load(jnp.int32(step)).start()
+    bbuf[z, x, c] = b_ref[0]
+    cbuf[c] = jnp.concatenate([c_ref[0].astype(jnp.float32), jnp.zeros((6, RANK), jnp.float32)], axis=0)
+    acc[...] = jnp.zeros_like(acc)
+    gacc[...] = jnp.zeros_like(gacc)
+    pl.semaphore_wait(barrier, len(partners))
+
+    own = bbuf.at[z, x, c]
+    for dx in (1, 3):
+        send(own, own, g_send.at[0], g_recv.at[0], at(dx=dx))
+    for dz in (1, 7):
+        send(own, own, z_send, z_recv.at[Z - dz], at(dz=dz))
+    send(own, own, g_send.at[0], g_recv.at[0], at(dx=2))
+    for dz in (2, 6, 3, 5, 4):
+        send(own, own, z_send, z_recv.at[Z - dz], at(dz=dz))
+    send(cbuf.at[c], cbuf.at[c], c_send, c_recv, peer)
+
+    def group(dz):
+        return bbuf.at[lax.rem(z + dz, Z), 0:3, c]
+
+    def relay(step, _):
+        dz = distance(step)
+        zz = lax.rem(z + dz, Z)
+        piece = bbuf.at[zz, x, c]
+        arrived(piece, z_recv.at[dz])
+        send(piece, piece, g_send.at[dz], g_recv.at[dz], at(dx=1))
+        send(piece, piece, g_send.at[dz], g_recv.at[dz], at(dx=3))
+        half = bbuf.at[zz, x, c, 0:32]
+        send(half, half, g_send.at[dz], g_recv.at[dz], at(dx=2))
+        return 0
+
+    def to_peer(dz):
+        part = bbuf.at[lax.rem(z + dz, Z), :, c]
+        send(part, part, k_send, k_recv.at[dz], peer)
+
+    lax.fori_loop(1, 3, relay, 0)
+    arrived(group(0), g_recv.at[0])
+    half = bbuf.at[z, lax.rem(x + 2, X), c, 32:64]
+    for dz in (1, 7, 2, 6, 3, 5, 4):
+        send(half, half, g_send.at[dz], g_recv.at[Z - dz], at(dz=dz))
+    to_peer(0)
+    lax.fori_loop(3, Z, relay, 0)
+
+    def own_group(step):
+        dz = distance(step)
+        arrived(group(dz), g_recv.at[dz])
+        to_peer(dz)
+
+    def gram_part(step):
+        dz = distance(step)
+        zz = lax.rem(z + dz, Z)
+        arrived(bbuf.at[zz, :, 1 - c], k_recv.at[dz])
+        block = bbuf[zz].reshape(512, RANK)
+        mine = bbuf[zz, :, :, :, pl.ds(pl.multiple_of(c * 128, 128), 128)].reshape(512, 128)
+        gacc[...] += lax.dot_general(
+            mine, block, (((0,), (0,)), ((), ())), preferred_element_type=jnp.float32
+        ).reshape(Y, 32, RANK)
+
+    def product(step):
+        zz = lax.rem(z + distance(step), Z)
+        load(step).wait()
+        block = bbuf[zz].reshape(512, RANK)
+        acc[...] += jnp.dot(
+            xbuf[zz].reshape(1024, 512), block, preferred_element_type=jnp.float32
+        )
+
+    def chunk(step, _):
+        own_group(step + 1)
+        gram_part(step)
+        product(step)
+        return 0
+
+    lax.fori_loop(0, Z - 1, chunk, 0)
+    gram_part(jnp.int32(Z - 1))
+    for dy in (1, 3, 2):
+        send(gacc.at[lax.rem(y + dy, Y)], grecv.at[Y - dy - 1], gs_send, gs_recv.at[Y - dy - 1], at(dy=dy))
+    product(jnp.int32(Z - 1))
+    rows = c_ref[0].astype(jnp.float32)
+    mixed = acc[0:512] * rows[0:1] + acc[512:1024] * rows[1:2]
+    comb[...] = mixed.reshape(Y, CORES, PIECE, RANK)
+    send(comb.at[:, 1 - c], ccore, mc_send, mc_recv, peer)
+
+    for d in range(3):
+        arrived(grecv.at[d], gs_recv.at[d])
+    gsum[...] = gacc[y] + grecv[0] + grecv[1] + grecv[2]
+    for dy in (1, 3, 2):
+        for core in (c, 1 - c):
+            send(gsum, gall.at[c * Y + y], ga_send, ga_recv, at(dy=dy, core=core))
+    send(gsum, gall.at[c * Y + y], ga_send, ga_recv, peer)
+
+    arrived(ccore, mc_recv)
+    csum[...] = ccore[...] + comb[:, c]
+    for dy in (1, 3, 2):
+        send(csum.at[lax.rem(y + dy, Y)], crecv_y.at[Y - dy - 1], my_send, my_recv.at[Y - dy - 1], at(dy=dy))
+    arrived(cbuf.at[1 - c], c_recv)
+    c_out[...] = cbuf[...].reshape(16, RANK)
+    arrived(gall.at[0:7], ga_recv)
+    gall[c * Y + y] = gsum[...]
+    gram_out[...] = gall[...].reshape(RANK, RANK)
+    for d in range(3):
+        arrived(crecv_y.at[d], my_recv.at[d])
+    m_out[...] = csum[y] + crecv_y[0] + crecv_y[1] + crecv_y[2]
+
+    def sent(ref, sem):
+        pltpu.make_async_remote_copy(
+            src_ref=ref, dst_ref=ref, send_sem=sem, recv_sem=sem, device_id=peer, device_id_type=MESH
+        ).wait_send()
+
+    sent(bbuf.at[0:7, 0, c], z_send)
+    for dz in range(Z):
+        sent(group(dz), g_send.at[dz])
+    sent(bbuf.at[:, :, c], k_send)
+    sent(cbuf.at[c], c_send)
+    sent(grecv, gs_send)
+    sent(gall.at[0:7], ga_send)
+    sent(ccore, mc_send)
+    sent(crecv_y, my_send)
+
+
 def per_device(tensor, factor_b, factor_c):
-    block = lax.all_gather(factor_b, ("ia", "ka"), axis=1, tiled=True)[0]
-    gram = lax.dot_general(
-        block, block, (((0,), (0,)), ((), ())), preferred_element_type=jnp.float32
-    )
-    gram = lax.psum(gram, "ja")
-    c_all = lax.all_gather(factor_c[0], "ka", axis=0, tiled=True)
-    slabs = jnp.einsum("kin,nr->kir", tensor, block, preferred_element_type=jnp.float32)
-    mttkrp = jnp.sum(slabs * factor_c[0].astype(jnp.float32)[:, None, :], axis=0)
-    rows = lax.psum_scatter(mttkrp, ("ja", "ka"), scatter_dimension=0, tiled=True)
+    f32, bf16 = jnp.float32, jnp.bfloat16
+    vmem = pl.BlockSpec(memory_space=pltpu.VMEM)
+    dma = pltpu.SemaphoreType.DMA
+    gram, c_all, rows = pl.pallas_call(
+        gather_kernel,
+        out_shape=(
+            jax.ShapeDtypeStruct((RANK, RANK), f32),
+            jax.ShapeDtypeStruct((16, RANK), f32),
+            jax.ShapeDtypeStruct((PIECE, RANK), f32),
+        ),
+        in_specs=[pl.BlockSpec(memory_space=pl.ANY), vmem, vmem],
+        out_specs=(vmem, vmem, vmem),
+        scratch_shapes=[
+            pltpu.VMEM((Z, 2, 512, 512), bf16),
+            pltpu.VMEM((Z, X, CORES, PIECE, RANK), bf16),
+            pltpu.VMEM((1024, RANK), f32),
+            pltpu.VMEM((Y, 32, RANK), f32),
+            pltpu.VMEM((3, 32, RANK), f32),
+            pltpu.VMEM((32, RANK), f32),
+            pltpu.VMEM((8, 32, RANK), f32),
+            pltpu.VMEM((CORES, 8, RANK), f32),
+            pltpu.VMEM((Y, CORES, PIECE, RANK), f32),
+            pltpu.VMEM((Y, PIECE, RANK), f32),
+            pltpu.VMEM((Y, PIECE, RANK), f32),
+            pltpu.VMEM((3, PIECE, RANK), f32),
+            dma((Z,)), dma, dma((Z,)), dma((Z,)), dma((Z,)), dma, dma((Z,)), dma, dma,
+            dma, dma((3,)), dma, dma, dma, dma, dma, dma((3,)),
+        ],
+        compiler_params=pltpu.CompilerParams(
+            collective_id=0, has_side_effects=True, vmem_limit_bytes=48 * 2**20
+        ),
+        cost_estimate=pl.CostEstimate(flops=2**31, bytes_accessed=2**23, transcendentals=0),
+        name="contract",
+    )(tensor, factor_b, factor_c)
     out = pl.pallas_call(
-        solve_kernel, out_shape=jax.ShapeDtypeStruct(rows.shape, jnp.float32), name="solve"
+        solve_kernel, out_shape=jax.ShapeDtypeStruct(rows.shape, f32), name="solve"
     )(gram, c_all, rows)
     return out[None]
 

time: 198 us -> 56.7 us (0.29)
  waiting for transfers between devices: 154 us -> 0 us
  Pallas kernels: 15.4 us -> 53.2 us
  between operations: 13.1 us -> 0.02 us
  matrix products: 10.4 us -> 0 us
  local copies, waits for them, and re-layouts: 0.61 us -> 3.35 us
    all_gather x1 -> x0, waiting for transfers between devices: 83.6 us -> none  [per_device(): block = lax.all_gather(factor_b, ('ia', 'ka'), axis=1, tiled=True)[0]]
    pallas_call x1 -> x2, Pallas kernels: 15.4 us -> 53.2 us  [the longest x1 37.8 us: per_device(): pl.pallas_call(gather_kernel, out_shape=(jax.ShapeDtypeStruct((RANK, RANK...]
    reduce_scatter x1 -> x0, waiting for transfers between devices: 36.5 us -> none  [per_device(): lax.psum_scatter(mttkrp, ('ja', 'ka'), scatter_dimension=0, tiled=True)]
    psum x1 -> x0, waiting for transfers between devices: 33.1 us -> none  [per_device(): gram = lax.psum(gram, 'ja')]
    dot_general x2 -> x0, matrix products: 10.4 us -> none  [the longest x1 6.56 us: per_device(): jnp.einsum('kin,nr->kir', tensor, block, preferred_element_type=jnp.float32)]
    unnamed x6 -> x10, local copies, waits for them, and re-layouts: 0.61 us -> 3.35 us
  transfers between devices with their start and end apart: 3 -> 0, of which waited for: 3 -> 0; matrix products, arithmetic and copies ran while one was open for 4% -> 0% of each run, Pallas kernels for 0% -> 0%
where the time goes in v2:
time: 56.7 us; the launch traced here: 56.6 us
  Pallas kernels  53.2 us (94%)
  local copies, waits for them, and re-layouts  3.35 us (6%)
    pallas_call x1, Pallas kernels, per_device(): pl.pallas_call(gather_kernel, out_shape=(jax.ShapeDtypeStruct((RANK, RANK...  37.8 us
    pallas_call x1, Pallas kernels, per_device(): pl.pallas_call(solve_kernel, out_shape=jax.ShapeDtypeStruct(rows.shape, f...  15.4 us
    unnamed x10, local copies, waits for them, and re-layouts  3.35 us

profile of v2, /device:TPU:1, one launch (start us, length us, event | category | flops | bytes accessed | tf_op | source)
XLA Modules:
  0.0 56.6 jit_solution(55369305274243302)
XLA Ops:
  0.0 0.0 copy-start.2
  0.0 0.8 %copy-done.2 = bf16[1,64,256]{2,1,0:T(8,128)(2,1)S(1)} copy-done((bf16[1,64,256]{2,1,0:T(8,128)(2,1)S(1)}, bf16[1,64,256]{2,1,0:T(8,128)(2,1)}, u32[]{:S(2)}) %copy-start.2) | copy-done | bytes 32792
  0.8 0.0 copy-start.4
  0.8 0.7 %copy-done.4 = bf16[1,2,256]{2,1,0:T(2,128)(2,1)S(1)} copy-done((bf16[1,2,256]{2,1,0:T(2,128)(2,1)S(1)}, bf16[1,2,256]{2,1,0:T(2,128)(2,1)}, u32[]{:S(2)}) %copy-start.4) | copy-done | bytes 1048
  1.4 37.8 %contract.1 = (f32[256,256]{1,0:T(8,128)S(1)}, f32[16,256]{1,0:T(8,128)S(1)}, f32[64,256]{1,0:T(8,128)S(1)}) custom-call(bf16[2,512,4096]{2,1,0:T(8,128)(2,1)} %x_hbm.1, bf16[1,64,256]{2,1,0:T(8,128)(2,1)S(1)} %copy-done.2, bf16[1,2,256]{2,1,0:T(2,128)(2,1)S(1)} %copy-done.4), custom_call_target="tpu_custom_call" | custom-call | flops 2147483648 | bytes 8388608 | tf_op jit(solution)/shard_map/contract/pallas_call | solution.py:242
  39.2 0.0 copy-start
  39.2 0.7 %copy-done = f32[256,256]{1,0:T(8,128)} copy-done((f32[256,256]{1,0:T(8,128)}, f32[256,256]{1,0:T(8,128)S(1)}, u32[]{:S(2)}) %copy-start) | copy-done | bytes 262168
  39.9 0.0 copy-start.1
  39.9 0.6 %copy-done.1 = f32[64,256]{1,0:T(8,128)} copy-done((f32[64,256]{1,0:T(8,128)}, f32[64,256]{1,0:T(8,128)S(1)}, u32[]{:S(2)}) %copy-start.1) | copy-done | bytes 65560
  40.6 0.0 copy-start.3
  40.6 0.6 %copy-done.3 = f32[16,256]{1,0:T(8,128)} copy-done((f32[16,256]{1,0:T(8,128)}, f32[16,256]{1,0:T(8,128)S(1)}, u32[]{:S(2)}) %copy-start.3) | copy-done | bytes 16408
  41.2 15.4 %solve.1 = f32[64,256]{1,0:T(8,128)} custom-call(f32[256,256]{1,0:T(8,128)} %copy-done, f32[16,256]{1,0:T(8,128)} %copy-done.3, f32[64,256]{1,0:T(8,128)} %copy-done.1), custom_call_target="tpu_custom_call" | custom-call | tf_op jit(solution)/shard_map/solve/pallas_call | solution.py:273
Async XLA Ops:
  0.0 0.8 %copy-start.2 = (bf16[1,64,256]{2,1,0:T(8,128)(2,1)S(1)}, bf16[1,64,256]{2,1,0:T(8,128)(2,1)}, u32[]{:S(2)}) copy-start(bf16[1,64,256]{2,1,0:T(8,128)(2,1)} %b_ref.1) | copy-start | bytes 98308
  0.8 0.7 %copy-start.4 = (bf16[1,2,256]{2,1,0:T(2,128)(2,1)S(1)}, bf16[1,2,256]{2,1,0:T(2,128)(2,1)}, u32[]{:S(2)}) copy-start(bf16[1,2,256]{2,1,0:T(2,128)(2,1)} %c_ref.1) | copy-start | bytes 3076
  39.2 0.7 %copy-start = (f32[256,256]{1,0:T(8,128)}, f32[256,256]{1,0:T(8,128)S(1)}, u32[]{:S(2)}) copy-start(f32[256,256]{1,0:T(8,128)S(1)} %get-tuple-element.8.gb_ref) | copy-start | bytes 786436
  39.9 0.6 %copy-start.1 = (f32[64,256]{1,0:T(8,128)}, f32[64,256]{1,0:T(8,128)S(1)}, u32[]{:S(2)}) copy-start(f32[64,256]{1,0:T(8,128)S(1)} %get-tuple-element.10.m_ref) | copy-start | bytes 196612
  40.6 0.6 %copy-start.3 = (f32[16,256]{1,0:T(8,128)}, f32[16,256]{1,0:T(8,128)S(1)}, u32[]{:S(2)}) copy-start(f32[16,256]{1,0:T(8,128)S(1)} %get-tuple-element.9.c_ref) | copy-start | bytes 49156

commit v3 on v2

v3 whole, which is shorter than its diff:
```python
import jax, jax.numpy as jnp
from jax import lax
from jax.experimental import pallas as pl
from jax.experimental.pallas import tpu as pltpu
from jax.sharding import PartitionSpec as P
HI=lax.Precision.HIGHEST


def dot(a,b,ta=False,tb=False):
    return lax.dot_general(a,b,(((0 if ta else 1,),(1 if tb else 0,)),((),())),precision=HI,preferred_element_type=jnp.float32)


def gj128(block, hook=None):
    tiles=[block[8*q:8*q+8,:] for q in range(16)]
    lane=lax.broadcasted_iota(jnp.int32,(8,128),1)
    sub=lax.broadcasted_iota(jnp.int32,(8,128),0)
    lb=lambda v,k: jnp.broadcast_to(v[:,k:k+1],(8,128))
    sb=lambda v,i: jnp.broadcast_to(v[i:i+1,:],(8,128))
    for p in range(16):
        if hook is not None:
            hook(p)
        cols=[lb(tiles[p],8*p+m) for m in range(8)]
        for s in range(4):
            i0,i1=2*s,2*s+1
            k0,k1=8*p+i0,8*p+i1
            c0,c1=cols[i0],cols[i1]
            a,b,d=sb(c0,i0),sb(c1,i0),sb(c1,i1)
            r=1.0/(a*d-b*b)
            at0,at1=lane==k0,lane==k1
            either=at0|at1
            rows=(sub==i0)|(sub==i1)
            e0=jnp.where(sub==i0,-1.0,jnp.where(sub==i1,0.0,c0))
            e1=jnp.where(sub==i1,-1.0,jnp.where(sub==i0,0.0,c1))
            T=tiles[p]
            row0,row1=sb(T,i0),sb(T,i1)
            w0=jnp.where(at0,-d,jnp.where(at1,b,d*row0-b*row1))*r
            w1=jnp.where(at0,b,jnp.where(at1,-a,a*row1-b*row0))*r
            for m in range(i1+1,8):
                t0,t1=sb(cols[m],i0),sb(cols[m],i1)
                g=e0*(d*t0-b*t1)+e1*(a*t1-b*t0)
                cols[m]=jnp.where(rows,0.0,cols[m])-g*r
            new=[]
            for q in range(16):
                t=tiles[q]
                if q==p:
                    new.append(jnp.where(either|rows,0.0,t)-e0*w0-e1*w1)
                else:
                    new.append(jnp.where(either,0.0,t)-lb(t,k0)*w0-lb(t,k1)*w1)
            tiles=new
    return -jnp.concatenate(tiles,axis=0)


Z, X, Y, CORES = 8, 4, 4, 2
PIECE = 64
RANK = 256
MESH = pl.DeviceIdType.MESH


def distance(step):
    return lax.rem(step, 2) * ((step + 1) // 2) + (1 - lax.rem(step, 2)) * lax.rem(Z - step // 2, Z)


def als_kernel(
    x_hbm, b_hbm, c_ref, out_ref,
    xbuf, bbuf, acc, cbuf, gpart, gxy, gz, gslice, gall, comb, ccore, csum, my,
    x_sem, b_sem, z_send, z_recv, g_send, g_recv, k_send, k_recv, o_send, o_recv, c_send, c_recv,
    gxy_send, gxy_recv, gz_send, gz_recv, ga_send, ga_recv, gp_send, gp_recv,
    mc_send, mc_recv, my_send, my_recv,
):
    ia, y, c = lax.axis_index("ia"), lax.axis_index("ja"), lax.axis_index("ka")
    z, x = ia // X, lax.rem(ia, X)
    peer = (ia, y, 1 - c)
    slot = y * X + x

    def at(dz=0, dx=0, dy=0):
        zz, xx = lax.rem(z + dz, Z), lax.rem(x + dx, X)
        return (zz * X + xx, lax.rem(y + dy, Y), c)

    def send(src, dst, ss, rs, to):
        copy = pltpu.make_async_remote_copy(
            src_ref=src, dst_ref=dst, send_sem=ss, recv_sem=rs, device_id=to, device_id_type=MESH
        )
        copy.start()

    def arrived(ref, sem):
        pltpu.make_async_remote_copy(
            src_ref=ref, dst_ref=ref, send_sem=sem, recv_sem=sem, device_id=peer, device_id_type=MESH
        ).wait_recv()

    def sent(ref, sem):
        pltpu.make_async_remote_copy(
            src_ref=ref, dst_ref=ref, send_sem=sem, recv_sem=sem, device_id=peer, device_id_type=MESH
        ).wait_send()

    def load(step):
        zz = lax.rem(z + distance(step), Z)
        return pltpu.make_async_copy(
            x_hbm.at[:, :, pl.ds(pl.multiple_of(zz * 512, 512), 512)], xbuf.at[zz], x_sem.at[step]
        )

    plane = [(dx, dy) for dy in (0, 1, 3, 2) for dx in (0, 1, 3, 2) if dx or dy]
    partners = [at(dz=d) for d in range(1, Z)] + [at(dx=dx, dy=dy) for dx, dy in plane] + [peer]
    barrier = pltpu.get_barrier_semaphore()
    for to in partners:
        pl.semaphore_signal(barrier, inc=1, device_id=to, device_id_type=MESH)
    own = bbuf.at[z, x, c]
    own_load = pltpu.make_async_copy(b_hbm.at[0], own, b_sem)
    own_load.start()
    for step in range(Z):
        load(jnp.int32(step)).start()
    cbuf[c] = jnp.concatenate([c_ref[0].astype(jnp.float32), jnp.zeros((6, RANK), jnp.float32)], axis=0)
    acc[...] = jnp.zeros_like(acc)
    own_load.wait()
    pl.semaphore_wait(barrier, len(partners))

    send(own, own, o_send, o_recv, peer)
    for dz in (1, 7, 2, 6, 3, 5, 4):
        send(own, own, z_send, z_recv.at[Z - dz], at(dz=dz))
    send(cbuf.at[c], cbuf.at[c], c_send, c_recv, peer)

    arrived(bbuf.at[z, x, 1 - c], o_recv)
    mine = bbuf[z, x, :, :, pl.ds(pl.multiple_of(c * 128, 128), 128)].reshape(128, 128)
    gpart[...] = lax.dot_general(
        mine, bbuf[z, x].reshape(128, RANK), (((0,), (0,)), ((), ())), preferred_element_type=jnp.float32
    ).reshape(16, 8, RANK)
    for dx, dy in plane:
        target = lax.rem(y + dy, Y) * X + lax.rem(x + dx, X)
        send(gpart.at[target], gxy.at[slot], gxy_send, gxy_recv, at(dx=dx, dy=dy))
    for dx in (1, 3, 2):
        send(own, own, g_send.at[0], g_recv.at[0], at(dx=dx))
    gxy[slot] = gpart[slot]

    def group(dz):
        return bbuf.at[lax.rem(z + dz, Z), 0:3, c]

    def relay(step, _):
        dz = distance(step)
        zz = lax.rem(z + dz, Z)
        piece = bbuf.at[zz, x, c]
        arrived(piece, z_recv.at[dz])
        send(piece, piece, g_send.at[dz], g_recv.at[dz], at(dx=1))
        send(piece, piece, g_send.at[dz], g_recv.at[dz], at(dx=3))
        half = bbuf.at[zz, x, c, 0:32]
        send(half, half, g_send.at[dz], g_recv.at[dz], at(dx=2))
        return 0

    lax.fori_loop(1, 3, relay, 0)
    arrived(group(0), g_recv.at[0])
    half = bbuf.at[z, lax.rem(x + 2, X), c, 32:64]
    for dz in (1, 7, 2, 6, 3, 5, 4):
        send(half, half, g_send.at[dz], g_recv.at[Z - dz], at(dz=dz))
    for dx in (1, 3, 2):
        part = bbuf.at[z, lax.rem(x + dx, X), c]
        send(part, part, o_send, k_recv.at[0], peer)

    arrived(gxy.at[0:15], gxy_recv)
    gz[z] = jnp.sum(gxy[...], axis=0)
    for dz in (4, 3, 5, 2, 6, 1, 7):
        send(gz.at[z], gz.at[z], gz_send, gz_recv, at(dz=dz))
    lax.fori_loop(3, Z, relay, 0)

    def gram_over_plane():
        arrived(gz.at[0:7], gz_recv)
        gslice[...] = jnp.sum(gz[...], axis=0)
        for dx, dy in plane:
            send(gslice, gall.at[c, slot], ga_send, ga_recv, at(dx=dx, dy=dy))
        gall[c, slot] = gslice[...]

    def gram_to_peer():
        arrived(gall.at[c, 0:15], ga_recv)
        send(gall.at[c], gall.at[c], gp_send, gp_recv, peer)

    def chunk(step, _):
        dz = distance(step)
        zz = lax.rem(z + dz, Z)

        @pl.when(step < Z - 1)
        def _():
            later = distance(step + 1)
            arrived(group(later), g_recv.at[later])
            part = bbuf.at[lax.rem(z + later, Z), :, c]
            send(part, part, k_send, k_recv.at[later], peer)

        @pl.when(step == 1)
        def _():
            gram_over_plane()

        @pl.when(step == 5)
        def _():
            gram_to_peer()

        @pl.when(step == 0)
        def _():
            arrived(bbuf.at[z, 0:3, 1 - c], k_recv.at[0])

        @pl.when(step > 0)
        def _():
            arrived(bbuf.at[zz, :, 1 - c], k_recv.at[dz])

        load(step).wait()
        acc[...] += jnp.dot(
            xbuf[zz].reshape(1024, 512), bbuf[zz].reshape(512, RANK), preferred_element_type=jnp.float32
        )
        return 0

    lax.fori_loop(0, Z, chunk, 0)
    rows = c_ref[0].astype(jnp.float32)
    mixed = acc[0:512] * rows[0:1] + acc[512:1024] * rows[1:2]
    comb[...] = mixed.reshape(Y, CORES, PIECE, RANK)
    send(comb.at[:, 1 - c], ccore, mc_send, mc_recv, peer)

    arrived(cbuf.at[1 - c], c_recv)
    arrived(gall.at[1 - c], gp_recv)
    factor = cbuf[...].reshape(16, RANK).astype(jnp.bfloat16)
    n = gall[...].reshape(RANK, RANK) * lax.dot_general(
        factor, factor, (((0,), (0,)), ((), ())), preferred_element_type=jnp.float32
    )
    eye = lax.broadcasted_iota(jnp.int32, n.shape, 0) == lax.broadcasted_iota(jnp.int32, n.shape, 1)
    diag = jnp.where(eye, n, 0.0)
    sr = lax.rsqrt(jnp.sum(diag, axis=0, keepdims=True))
    sc = lax.rsqrt(jnp.sum(diag, axis=1, keepdims=True))
    n = n * sr * sc
    n11, n12, n22 = n[:128, :128], n[:128, 128:], n[128:, 128:]

    def hook(p):
        if p != 4:
            return
        arrived(ccore, mc_recv)
        csum[...] = ccore[...] + comb[:, c]
        for dy in (1, 3, 2):
            send(csum.at[lax.rem(y + dy, Y)], my.at[y], my_send, my_recv, at(dy=dy))
        my[y] = csum[y]

    i1 = gj128(n11, hook)
    t = dot(i1, n12)
    i2 = gj128(n22 - dot(n12, t, ta=True))
    arrived(my.at[0:3], my_recv)
    m = jnp.sum(my[...], axis=0) * sr
    m1, m2 = m[:, :128], m[:, 128:]
    last = dot(m2 - dot(m1, t), i2)
    first = dot(m1, i1) - dot(last, t, tb=True)
    out_ref[0] = jnp.concatenate([first, last], axis=1) * sr

    sent(bbuf.at[z, :, c], o_send)
    sent(bbuf.at[0:7, 0, c], z_send)
    for dz in range(Z):
        sent(group(dz), g_send.at[dz])
    sent(bbuf.at[0:7, :, c], k_send)
    sent(cbuf.at[c], c_send)
    sent(gxy.at[0:15], gxy_send)
    sent(gz.at[0:7], gz_send)
    sent(gxy.at[0:15], ga_send)
    sent(gall.at[c], gp_send)
    sent(ccore, mc_send)
    sent(my.at[0:3], my_send)


def per_device(tensor, factor_b, factor_c):
    f32, bf16 = jnp.float32, jnp.bfloat16
    vmem = pl.BlockSpec(memory_space=pltpu.VMEM)
    hbm = pl.BlockSpec(memory_space=pl.ANY)
    dma = pltpu.SemaphoreType.DMA
    return pl.pallas_call(
        als_kernel,
        out_shape=jax.ShapeDtypeStruct((1, PIECE, RANK), f32),
        in_specs=[hbm, hbm, vmem],
        out_specs=vmem,
        scratch_shapes=[
            pltpu.VMEM((Z, 2, 512, 512), bf16),
            pltpu.VMEM((Z, X, CORES, PIECE, RANK), bf16),
            pltpu.VMEM((1024, RANK), f32),
            pltpu.VMEM((CORES, 8, RANK), f32),
            pltpu.VMEM((16, 8, RANK), f32),
            pltpu.VMEM((16, 8, RANK), f32),
            pltpu.VMEM((Z, 8, RANK), f32),
            pltpu.VMEM((8, RANK), f32),
            pltpu.VMEM((CORES, 16, 8, RANK), f32),
            pltpu.VMEM((Y, CORES, PIECE, RANK), f32),
            pltpu.VMEM((Y, PIECE, RANK), f32),
            pltpu.VMEM((Y, PIECE, RANK), f32),
            pltpu.VMEM((Y, PIECE, RANK), f32),
            dma((Z,)), dma, dma, dma((Z,)), dma((Z,)), dma((Z,)), dma, dma((Z,)), dma, dma, dma, dma,
            dma, dma, dma, dma, dma, dma, dma, dma, dma, dma, dma, dma,
        ],
        compiler_params=pltpu.CompilerParams(
            collective_id=0, has_side_effects=True, vmem_limit_bytes=48 * 2**20
        ),
        cost_estimate=pl.CostEstimate(flops=2**31, bytes_accessed=2**23, transcendentals=0),
        name="als",
    )(tensor, factor_b, factor_c)


def solution(mesh):
    return jax.shard_map(
        per_device,
        mesh=mesh,
        in_specs=(P("ka", "ia", "ja"), P("ja", ("ia", "ka"), None), P("ka", None, None)),
        out_specs=P("ia", ("ja", "ka"), None),
        check_vma=False,
    )
```

time: 56.7 us -> 54.6 us (0.963)
  local copies, waits for them, and re-layouts: 3.35 us -> 2.07 us
  Pallas kernels: 53.2 us -> 52.3 us
    unnamed x10 -> x5, local copies, waits for them, and re-layouts: 3.35 us -> 2.07 us
    pallas_call x2 -> x1, Pallas kernels: 53.2 us -> 52.3 us  [per_device(): pl.pallas_call(als_kernel, out_shape=jax.ShapeDtypeStruct((1, PIECE, RANK...]
where the time goes in v3:
time: 54.6 us; the launch traced here: 54.4 us
  Pallas kernels  52.3 us (96%)
  local copies, waits for them, and re-layouts  2.07 us (4%)
    pallas_call x1, Pallas kernels, per_device(): pl.pallas_call(als_kernel, out_shape=jax.ShapeDtypeStruct((1, PIECE, RANK...  52.3 us
    unnamed x5, local copies, waits for them, and re-layouts  2.07 us

profile of v3, /device:TPU:1, one launch (start us, length us, event | category | flops | bytes accessed | tf_op | source)
XLA Modules:
  0.0 54.4 jit_solution(18088173112774407676)
XLA Ops:
  0.0 0.0 copy-start
  0.0 0.8 %copy-done = bf16[1,64,256]{2,1,0:T(8,128)(2,1)S(1)} copy-done((bf16[1,64,256]{2,1,0:T(8,128)(2,1)S(1)}, bf16[1,64,256]{2,1,0:T(8,128)(2,1)}, u32[]{:S(2)}) %copy-start) | copy-done | bytes 32792
  0.8 0.0 copy-start.1
  0.8 0.7 %copy-done.1 = bf16[1,2,256]{2,1,0:T(2,128)(2,1)S(1)} copy-done((bf16[1,2,256]{2,1,0:T(2,128)(2,1)S(1)}, bf16[1,2,256]{2,1,0:T(2,128)(2,1)}, u32[]{:S(2)}) %copy-start.1) | copy-done | bytes 1048
  1.4 52.3 %als.1 = f32[1,64,256]{2,1,0:T(8,128)S(1)} custom-call(bf16[2,512,4096]{2,1,0:T(8,128)(2,1)} %x_hbm.1, bf16[1,64,256]{2,1,0:T(8,128)(2,1)S(1)} %copy-done, bf16[1,2,256]{2,1,0:T(2,128)(2,1)S(1)} %copy-done.1), custom_call_target="tpu_custom_call" | custom-call | flops 2147483648 | bytes 8388608 | tf_op jit(solution)/shard_map/als/pallas_call | solution.py:263
  53.8 0.6 %copy.5 = f32[1,64,256]{2,1,0:T(8,128)} copy(f32[1,64,256]{2,1,0:T(8,128)S(1)} %als.1) | data formatting | bytes 131072
Async XLA Ops:
  0.0 0.8 %copy-start = (bf16[1,64,256]{2,1,0:T(8,128)(2,1)S(1)}, bf16[1,64,256]{2,1,0:T(8,128)(2,1)}, u32[]{:S(2)}) copy-start(bf16[1,64,256]{2,1,0:T(8,128)(2,1)} %b_hbm.1) | copy-start | bytes 98308
  0.8 0.7 %copy-start.1 = (bf16[1,2,256]{2,1,0:T(2,128)(2,1)S(1)}, bf16[1,2,256]{2,1,0:T(2,128)(2,1)}, u32[]{:S(2)}) copy-start(bf16[1,2,256]{2,1,0:T(2,128)(2,1)} %c_ref.1) | copy-start | bytes 3076

commit v4 on v3

--- a/solution.py
+++ b/solution.py
@@ -10,44 +10,101 @@
     return lax.dot_general(a,b,(((0 if ta else 1,),(1 if tb else 0,)),((),())),precision=HI,preferred_element_type=jnp.float32)
 
 
-def gj128(block, hook=None):
-    tiles=[block[8*q:8*q+8,:] for q in range(16)]
-    lane=lax.broadcasted_iota(jnp.int32,(8,128),1)
-    sub=lax.broadcasted_iota(jnp.int32,(8,128),0)
-    lb=lambda v,k: jnp.broadcast_to(v[:,k:k+1],(8,128))
-    sb=lambda v,i: jnp.broadcast_to(v[i:i+1,:],(8,128))
-    for p in range(16):
+def split(v):
+    hi = v.astype(jnp.bfloat16)
+    rest = v - hi.astype(jnp.float32)
+    mid = rest.astype(jnp.bfloat16)
+    return hi, mid, (rest - mid.astype(jnp.float32)).astype(jnp.bfloat16)
+
+
+def invert(aref, hook=None):
+    lane = lax.broadcasted_iota(jnp.int32, (8, 128), 1)
+    sub = lax.broadcasted_iota(jnp.int32, (8, 128), 0)
+
+    def read(row):
+        return [aref[row : row + 8, 0:128], aref[row : row + 8, 128:256]]
+
+    def over_lanes(tile, k):
+        v = tile[k // 128]
+        return jnp.broadcast_to(v[:, k % 128 : k % 128 + 1], (8, 128))
+
+    def over_rows(v, i):
+        return jnp.broadcast_to(v[i : i + 1, :], (8, 128))
+
+    def eliminate(tile, first, done):
+        count = 8 * len(done)
+        half, off = first // 128, first % 128
+        spread = [over_lanes(tile, first + m) for m in range(count)]
+        new = []
+        for side in range(2):
+            parts = [spread[m] * over_rows(done[m // 8][side], m % 8) for m in range(count)]
+            while len(parts) > 1:
+                parts = [parts[i] + parts[i + 1] for i in range(0, len(parts), 2)]
+            kept = tile[side]
+            if side == half:
+                kept = jnp.where((lane >= off) & (lane < off + count), 0.0, kept)
+            new.append(kept - parts[0])
+        return new
+
+    tiles = [read(0), read(8)]
+    for panel in range(16):
         if hook is not None:
-            hook(p)
-        cols=[lb(tiles[p],8*p+m) for m in range(8)]
-        for s in range(4):
-            i0,i1=2*s,2*s+1
-            k0,k1=8*p+i0,8*p+i1
-            c0,c1=cols[i0],cols[i1]
-            a,b,d=sb(c0,i0),sb(c1,i0),sb(c1,i1)
-            r=1.0/(a*d-b*b)
-            at0,at1=lane==k0,lane==k1
-            either=at0|at1
-            rows=(sub==i0)|(sub==i1)
-            e0=jnp.where(sub==i0,-1.0,jnp.where(sub==i1,0.0,c0))
-            e1=jnp.where(sub==i1,-1.0,jnp.where(sub==i0,0.0,c1))
-            T=tiles[p]
-            row0,row1=sb(T,i0),sb(T,i1)
-            w0=jnp.where(at0,-d,jnp.where(at1,b,d*row0-b*row1))*r
-            w1=jnp.where(at0,b,jnp.where(at1,-a,a*row1-b*row0))*r
-            for m in range(i1+1,8):
-                t0,t1=sb(cols[m],i0),sb(cols[m],i1)
-                g=e0*(d*t0-b*t1)+e1*(a*t1-b*t0)
-                cols[m]=jnp.where(rows,0.0,cols[m])-g*r
-            new=[]
-            for q in range(16):
-                t=tiles[q]
-                if q==p:
-                    new.append(jnp.where(either|rows,0.0,t)-e0*w0-e1*w1)
-                else:
-                    new.append(jnp.where(either,0.0,t)-lb(t,k0)*w0-lb(t,k1)*w1)
-            tiles=new
-    return -jnp.concatenate(tiles,axis=0)
+            hook(panel)
+        base = 16 * panel
+        half, off = base // 128, base % 128
+        for h in range(2):
+            cols = [over_lanes(tiles[h], base + 8 * h + m) for m in range(8)]
+            for s in range(4):
+                i0, i1 = 2 * s, 2 * s + 1
+                k0, k1 = base + 8 * h + i0, base + 8 * h + i1
+                c0, c1 = cols[i0], cols[i1]
+                a, b, d = over_rows(c0, i0), over_rows(c1, i0), over_rows(c1, i1)
+                r = 1.0 / (a * d - b * b)
+                at0, at1 = lane == k0 % 128, lane == k1 % 128
+                either = at0 | at1
+                rows = (sub == i0) | (sub == i1)
+                e0 = jnp.where(sub == i0, -1.0, jnp.where(sub == i1, 0.0, c0))
+                e1 = jnp.where(sub == i1, -1.0, jnp.where(sub == i0, 0.0, c1))
+                for m in range(i1 + 1, 8):
+                    t0, t1 = over_rows(cols[m], i0), over_rows(cols[m], i1)
+                    g = e0 * (d * t0 - b * t1) + e1 * (a * t1 - b * t0)
+                    cols[m] = jnp.where(rows, 0.0, cols[m]) - g * r
+                mine = []
+                for side in range(2):
+                    T = tiles[h][side]
+                    row0, row1 = over_rows(T, i0), over_rows(T, i1)
+                    w0, w1 = d * row0 - b * row1, a * row1 - b * row0
+                    T = jnp.where(rows, 0.0, T)
+                    if side == half:
+                        w0 = jnp.where(at0, -d, jnp.where(at1, b, w0))
+                        w1 = jnp.where(at0, b, jnp.where(at1, -a, w1))
+                        T = jnp.where(either, 0.0, T)
+                    w0, w1 = w0 * r, w1 * r
+                    mine.append(T - e0 * w0 - e1 * w1)
+                tiles[h] = mine
+            tiles[1 - h] = eliminate(tiles[1 - h], base + 8 * h, [tiles[h]])
+        done = tiles
+        if panel < 15:
+            tiles = [eliminate(read(base + 16 + 8 * q), base, done) for q in range(2)]
+        w = jnp.concatenate([jnp.concatenate(t, axis=1) for t in done], axis=0)
+        wh, wm, wl = split(w)
+
+        def pad(v):
+            parts = [v]
+            if off:
+                parts.insert(0, jnp.zeros((off, 256), jnp.bfloat16))
+            if off < 112:
+                parts.append(jnp.zeros((112 - off, 256), jnp.bfloat16))
+            return jnp.concatenate(parts, axis=0) if len(parts) > 1 else v
+
+        hi, mid, lo = split(aref[:, 128 * half : 128 * half + 128])
+        both = jnp.concatenate([hi, mid], axis=1)
+        f = lambda l, r0, r1: jnp.dot(l, jnp.concatenate([pad(r0), pad(r1)], axis=0), preferred_element_type=jnp.float32)
+        change = f(both, wh, wh) + f(both, wm, wm) + f(jnp.concatenate([hi, lo], axis=1), wl, wh)
+        lanes = lax.broadcasted_iota(jnp.int32, (256, 256), 1)
+        keep = jnp.where((lanes >= base) & (lanes < base + 16), 0.0, aref[...])
+        aref[...] = keep - change
+        aref[base : base + 16, :] = w
 
 
 Z, X, Y, CORES = 8, 4, 4, 2
@@ -62,7 +119,7 @@
 
 def als_kernel(
     x_hbm, b_hbm, c_ref, out_ref,
-    xbuf, bbuf, acc, cbuf, gpart, gxy, gz, gslice, gall, comb, ccore, csum, my,
+    xbuf, bbuf, acc, cbuf, gpart, gxy, gz, gslice, gall, comb, ccore, csum, my, matrix,
     x_sem, b_sem, z_send, z_recv, g_send, g_recv, k_send, k_recv, o_send, o_recv, c_send, c_recv,
     gxy_send, gxy_recv, gz_send, gz_recv, ga_send, ga_recv, gp_send, gp_recv,
     mc_send, mc_recv, my_send, my_recv,
@@ -98,7 +155,7 @@
             x_hbm.at[:, :, pl.ds(pl.multiple_of(zz * 512, 512), 512)], xbuf.at[zz], x_sem.at[step]
         )
 
-    plane = [(dx, dy) for dy in (0, 1, 3, 2) for dx in (0, 1, 3, 2) if dx or dy]
+    plane = [(dx, dy) for dy in (2, 1, 3, 0) for dx in (2, 1, 3, 0) if dx or dy]
     partners = [at(dz=d) for d in range(1, Z)] + [at(dx=dx, dy=dy) for dx, dy in plane] + [peer]
     barrier = pltpu.get_barrier_semaphore()
     for to in partners:
@@ -219,27 +276,24 @@
     diag = jnp.where(eye, n, 0.0)
     sr = lax.rsqrt(jnp.sum(diag, axis=0, keepdims=True))
     sc = lax.rsqrt(jnp.sum(diag, axis=1, keepdims=True))
-    n = n * sr * sc
-    n11, n12, n22 = n[:128, :128], n[:128, 128:], n[128:, 128:]
-
-    def hook(p):
-        if p != 4:
+    matrix[...] = n * sr * sc
+
+    def hook(panel):
+        if panel != 3:
             return
-        arrived(ccore, mc_recv)
-        csum[...] = ccore[...] + comb[:, c]
-        for dy in (1, 3, 2):
-            send(csum.at[lax.rem(y + dy, Y)], my.at[y], my_send, my_recv, at(dy=dy))
-        my[y] = csum[y]
-
-    i1 = gj128(n11, hook)
-    t = dot(i1, n12)
-    i2 = gj128(n22 - dot(n12, t, ta=True))
+
+        @pl.when(ia >= 0)
+        def _():
+            arrived(ccore, mc_recv)
+            csum[...] = ccore[...] + comb[:, c]
+            for dy in (1, 3, 2):
+                send(csum.at[lax.rem(y + dy, Y)], my.at[y], my_send, my_recv, at(dy=dy))
+            my[y] = csum[y]
+
+    invert(matrix, hook)
     arrived(my.at[0:3], my_recv)
     m = jnp.sum(my[...], axis=0) * sr
-    m1, m2 = m[:, :128], m[:, 128:]
-    last = dot(m2 - dot(m1, t), i2)
-    first = dot(m1, i1) - dot(last, t, tb=True)
-    out_ref[0] = jnp.concatenate([first, last], axis=1) * sr
+    out_ref[0] = -dot(m, matrix[...]) * sr
 
     sent(bbuf.at[z, :, c], o_send)
     sent(bbuf.at[0:7, 0, c], z_send)
@@ -279,6 +333,7 @@
             pltpu.VMEM((Y, PIECE, RANK), f32),
             pltpu.VMEM((Y, PIECE, RANK), f32),
             pltpu.VMEM((Y, PIECE, RANK), f32),
+            pltpu.VMEM((RANK, RANK), f32),
             dma((Z,)), dma, dma, dma((Z,)), dma((Z,)), dma((Z,)), dma, dma((Z,)), dma, dma, dma, dma,
             dma, dma, dma, dma, dma, dma, dma, dma, dma, dma, dma, dma,
         ],

time: 54.6 us -> 42.3 us (0.77)
  Pallas kernels: 52.3 us -> 40 us
    pallas_call x1, Pallas kernels: 52.3 us -> 40 us  [per_device(): pl.pallas_call(als_kernel, out_shape=jax.ShapeDtypeStruct((1, PIECE, RANK...]
where the time goes in v4:
time: 42.3 us; the launch traced here: 42.1 us
  Pallas kernels  40 us (95%)
  local copies, waits for them, and re-layouts  2.07 us (5%)
    pallas_call x1, Pallas kernels, per_device(): pl.pallas_call(als_kernel, out_shape=jax.ShapeDtypeStruct((1, PIECE, RANK...  40 us
    unnamed x5, local copies, waits for them, and re-layouts  2.07 us

profile of v4, /device:TPU:1, one launch (start us, length us, event | category | flops | bytes accessed | tf_op | source)
XLA Modules:
  0.0 42.1 jit_solution(15861724996515299702)
XLA Ops:
  0.0 0.0 copy-start
  0.0 0.8 %copy-done = bf16[1,64,256]{2,1,0:T(8,128)(2,1)S(1)} copy-done((bf16[1,64,256]{2,1,0:T(8,128)(2,1)S(1)}, bf16[1,64,256]{2,1,0:T(8,128)(2,1)}, u32[]{:S(2)}) %copy-start) | copy-done | bytes 32792
  0.8 0.0 copy-start.1
  0.8 0.7 %copy-done.1 = bf16[1,2,256]{2,1,0:T(2,128)(2,1)S(1)} copy-done((bf16[1,2,256]{2,1,0:T(2,128)(2,1)S(1)}, bf16[1,2,256]{2,1,0:T(2,128)(2,1)}, u32[]{:S(2)}) %copy-start.1) | copy-done | bytes 1048
  1.4 40.0 %als.1 = f32[1,64,256]{2,1,0:T(8,128)S(1)} custom-call(bf16[2,512,4096]{2,1,0:T(8,128)(2,1)} %x_hbm.1, bf16[1,64,256]{2,1,0:T(8,128)(2,1)S(1)} %copy-done, bf16[1,2,256]{2,1,0:T(2,128)(2,1)S(1)} %copy-done.1), custom_call_target="tpu_custom_call" | custom-call | flops 2147483648 | bytes 8388608 | tf_op jit(solution)/shard_map/als/pallas_call | solution.py:317
  41.5 0.6 %copy.5 = f32[1,64,256]{2,1,0:T(8,128)} copy(f32[1,64,256]{2,1,0:T(8,128)S(1)} %als.1) | data formatting | bytes 131072
Async XLA Ops:
  0.0 0.8 %copy-start = (bf16[1,64,256]{2,1,0:T(8,128)(2,1)S(1)}, bf16[1,64,256]{2,1,0:T(8,128)(2,1)}, u32[]{:S(2)}) copy-start(bf16[1,64,256]{2,1,0:T(8,128)(2,1)} %b_hbm.1) | copy-start | bytes 98308
  0.8 0.7 %copy-start.1 = (bf16[1,2,256]{2,1,0:T(2,128)(2,1)S(1)}, bf16[1,2,256]{2,1,0:T(2,128)(2,1)}, u32[]{:S(2)}) copy-start(bf16[1,2,256]{2,1,0:T(2,128)(2,1)} %c_ref.1) | copy-start | bytes 3076

commit v5 on v4

--- a/solution.py
+++ b/solution.py
@@ -202,6 +202,10 @@
         return 0
 
     lax.fori_loop(1, 3, relay, 0)
+    arrived(gxy.at[0:15], gxy_recv)
+    gz[z] = jnp.sum(gxy[...], axis=0)
+    for dz in (4, 3, 5, 2, 6, 1, 7):
+        send(gz.at[z], gz.at[z], gz_send, gz_recv, at(dz=dz))
     arrived(group(0), g_recv.at[0])
     half = bbuf.at[z, lax.rem(x + 2, X), c, 32:64]
     for dz in (1, 7, 2, 6, 3, 5, 4):
@@ -210,10 +214,6 @@
         part = bbuf.at[z, lax.rem(x + dx, X), c]
         send(part, part, o_send, k_recv.at[0], peer)
 
-    arrived(gxy.at[0:15], gxy_recv)
-    gz[z] = jnp.sum(gxy[...], axis=0)
-    for dz in (4, 3, 5, 2, 6, 1, 7):
-        send(gz.at[z], gz.at[z], gz_send, gz_recv, at(dz=dz))
     lax.fori_loop(3, Z, relay, 0)
 
     def gram_over_plane():
@@ -238,11 +238,7 @@
             part = bbuf.at[lax.rem(z + later, Z), :, c]
             send(part, part, k_send, k_recv.at[later], peer)
 
-        @pl.when(step == 1)
-        def _():
-            gram_over_plane()
-
-        @pl.when(step == 5)
+        @pl.when(step == 7)
         def _():
             gram_to_peer()
 
@@ -260,6 +256,7 @@
         )
         return 0
 
+    gram_over_plane()
     lax.fori_loop(0, Z, chunk, 0)
     rows = c_ref[0].astype(jnp.float32)
     mixed = acc[0:512] * rows[0:1] + acc[512:1024] * rows[1:2]

time: 42.3 us -> 39.5 us (0.934)
  Pallas kernels: 40 us -> 37.3 us
    pallas_call x1, Pallas kernels: 40 us -> 37.3 us  [per_device(): pl.pallas_call(als_kernel, out_shape=jax.ShapeDtypeStruct((1, PIECE, RANK...]
where the time goes in v5:
time: 39.5 us; the launch traced here: 39.3 us
  Pallas kernels  37.3 us (94%)
  local copies, waits for them, and re-layouts  2.07 us (5%)
    pallas_call x1, Pallas kernels, per_device(): pl.pallas_call(als_kernel, out_shape=jax.ShapeDtypeStruct((1, PIECE, RANK...  37.3 us
    unnamed x5, local copies, waits for them, and re-layouts  2.07 us

profile of v5, /device:TPU:1, one launch (start us, length us, event | category | flops | bytes accessed | tf_op | source)
XLA Modules:
  0.0 39.3 jit_solution(1886640473307619198)
XLA Ops:
  0.0 0.0 copy-start
  0.0 0.8 %copy-done = bf16[1,64,256]{2,1,0:T(8,128)(2,1)S(1)} copy-done((bf16[1,64,256]{2,1,0:T(8,128)(2,1)S(1)}, bf16[1,64,256]{2,1,0:T(8,128)(2,1)}, u32[]{:S(2)}) %copy-start) | copy-done | bytes 32792
  0.8 0.0 copy-start.1
  0.8 0.7 %copy-done.1 = bf16[1,2,256]{2,1,0:T(2,128)(2,1)S(1)} copy-done((bf16[1,2,256]{2,1,0:T(2,128)(2,1)S(1)}, bf16[1,2,256]{2,1,0:T(2,128)(2,1)}, u32[]{:S(2)}) %copy-start.1) | copy-done | bytes 1048
  1.4 37.3 %als.1 = f32[1,64,256]{2,1,0:T(8,128)S(1)} custom-call(bf16[2,512,4096]{2,1,0:T(8,128)(2,1)} %x_hbm.1, bf16[1,64,256]{2,1,0:T(8,128)(2,1)S(1)} %copy-done, bf16[1,2,256]{2,1,0:T(2,128)(2,1)S(1)} %copy-done.1), custom_call_target="tpu_custom_call" | custom-call | flops 2147483648 | bytes 8388608 | tf_op jit(solution)/shard_map/als/pallas_call | solution.py:314
  38.7 0.6 %copy.5 = f32[1,64,256]{2,1,0:T(8,128)} copy(f32[1,64,256]{2,1,0:T(8,128)S(1)} %als.1) | data formatting | bytes 131072
Async XLA Ops:
  0.0 0.8 %copy-start = (bf16[1,64,256]{2,1,0:T(8,128)(2,1)S(1)}, bf16[1,64,256]{2,1,0:T(8,128)(2,1)}, u32[]{:S(2)}) copy-start(bf16[1,64,256]{2,1,0:T(8,128)(2,1)} %b_hbm.1) | copy-start | bytes 98308
  0.8 0.7 %copy-start.1 = (bf16[1,2,256]{2,1,0:T(2,128)(2,1)S(1)}, bf16[1,2,256]{2,1,0:T(2,128)(2,1)}, u32[]{:S(2)}) copy-start(bf16[1,2,256]{2,1,0:T(2,128)(2,1)} %c_ref.1) | copy-start | bytes 3076

commit v6 on v5

--- a/solution.py
+++ b/solution.py
@@ -8,6 +8,9 @@
 
 def dot(a,b,ta=False,tb=False):
     return lax.dot_general(a,b,(((0 if ta else 1,),(1 if tb else 0,)),((),())),precision=HI,preferred_element_type=jnp.float32)
+
+
+NEAR = 3
 
 
 def split(v):
@@ -65,22 +68,25 @@
                 rows = (sub == i0) | (sub == i1)
                 e0 = jnp.where(sub == i0, -1.0, jnp.where(sub == i1, 0.0, c0))
                 e1 = jnp.where(sub == i1, -1.0, jnp.where(sub == i0, 0.0, c1))
+                q0, q1 = (d * e0 - b * e1) * r, (a * e1 - b * e0) * r
                 for m in range(i1 + 1, 8):
                     t0, t1 = over_rows(cols[m], i0), over_rows(cols[m], i1)
-                    g = e0 * (d * t0 - b * t1) + e1 * (a * t1 - b * t0)
-                    cols[m] = jnp.where(rows, 0.0, cols[m]) - g * r
+                    kept = jnp.where(rows, 0.0, cols[m])
+                    if m < i1 + NEAR:
+                        g = e0 * (d * t0 - b * t1) + e1 * (a * t1 - b * t0)
+                        cols[m] = kept - g * r
+                    else:
+                        cols[m] = kept - (q0 * t0 + q1 * t1)
                 mine = []
                 for side in range(2):
                     T = tiles[h][side]
                     row0, row1 = over_rows(T, i0), over_rows(T, i1)
-                    w0, w1 = d * row0 - b * row1, a * row1 - b * row0
                     T = jnp.where(rows, 0.0, T)
                     if side == half:
-                        w0 = jnp.where(at0, -d, jnp.where(at1, b, w0))
-                        w1 = jnp.where(at0, b, jnp.where(at1, -a, w1))
+                        row0 = jnp.where(at0, -1.0, jnp.where(at1, 0.0, row0))
+                        row1 = jnp.where(at1, -1.0, jnp.where(at0, 0.0, row1))
                         T = jnp.where(either, 0.0, T)
-                    w0, w1 = w0 * r, w1 * r
-                    mine.append(T - e0 * w0 - e1 * w1)
+                    mine.append(T - (q0 * row0 + q1 * row1))
                 tiles[h] = mine
             tiles[1 - h] = eliminate(tiles[1 - h], base + 8 * h, [tiles[h]])
         done = tiles
@@ -98,12 +104,19 @@
             return jnp.concatenate(parts, axis=0) if len(parts) > 1 else v
 
         hi, mid, lo = split(aref[:, 128 * half : 128 * half + 128])
-        both = jnp.concatenate([hi, mid], axis=1)
-        f = lambda l, r0, r1: jnp.dot(l, jnp.concatenate([pad(r0), pad(r1)], axis=0), preferred_element_type=jnp.float32)
-        change = f(both, wh, wh) + f(both, wm, wm) + f(jnp.concatenate([hi, lo], axis=1), wl, wh)
-        lanes = lax.broadcasted_iota(jnp.int32, (256, 256), 1)
-        keep = jnp.where((lanes >= base) & (lanes < base + 16), 0.0, aref[...])
-        aref[...] = keep - change
+        change = jnp.dot(
+            jnp.concatenate([hi, mid, hi, mid, hi, lo], axis=1),
+            jnp.concatenate([pad(v) for v in (wh, wh, wm, wm, wl, wh)], axis=0),
+            preferred_element_type=jnp.float32,
+        )
+        lanes = lax.broadcasted_iota(jnp.int32, (256, 128), 1)
+        inside = (lanes >= off) & (lanes < off + 16)
+        for side in range(2):
+            span = slice(128 * side, 128 * side + 128)
+            kept = aref[:, span]
+            if side == half:
+                kept = jnp.where(inside, 0.0, kept)
+            aref[:, span] = kept - change[:, span]
         aref[base : base + 16, :] = w
 
 
@@ -264,11 +277,12 @@
     send(comb.at[:, 1 - c], ccore, mc_send, mc_recv, peer)
 
     arrived(cbuf.at[1 - c], c_recv)
-    arrived(gall.at[1 - c], gp_recv)
     factor = cbuf[...].reshape(16, RANK).astype(jnp.bfloat16)
-    n = gall[...].reshape(RANK, RANK) * lax.dot_general(
+    matrix[...] = lax.dot_general(
         factor, factor, (((0,), (0,)), ((), ())), preferred_element_type=jnp.float32
     )
+    arrived(gall.at[1 - c], gp_recv)
+    n = gall[...].reshape(RANK, RANK) * matrix[...]
     eye = lax.broadcasted_iota(jnp.int32, n.shape, 0) == lax.broadcasted_iota(jnp.int32, n.shape, 1)
     diag = jnp.where(eye, n, 0.0)
     sr = lax.rsqrt(jnp.sum(diag, axis=0, keepdims=True))
@@ -276,7 +290,7 @@
     matrix[...] = n * sr * sc
 
     def hook(panel):
-        if panel != 3:
+        if panel != 1:
             return
 
         @pl.when(ia >= 0)

time: 39.5 us -> 39.1 us (0.990)
  Pallas kernels: 37.3 us -> 36.8 us
    pallas_call x1, Pallas kernels: 37.3 us -> 36.8 us  [per_device(): pl.pallas_call(als_kernel, out_shape=jax.ShapeDtypeStruct((1, PIECE, RANK...]
where the time goes in v6:
time: 39.1 us; the launch traced here: 38.9 us
  Pallas kernels  36.8 us (94%)
  local copies, waits for them, and re-layouts  2.07 us (5%)
    pallas_call x1, Pallas kernels, per_device(): pl.pallas_call(als_kernel, out_shape=jax.ShapeDtypeStruct((1, PIECE, RANK...  36.8 us
    unnamed x5, local copies, waits for them, and re-layouts  2.07 us

profile of v6, /device:TPU:1, one launch (start us, length us, event | category | flops | bytes accessed | tf_op | source)
XLA Modules:
  0.0 38.9 jit_solution(9124685230796043331)
XLA Ops:
  0.0 0.0 copy-start
  0.0 0.8 %copy-done = bf16[1,64,256]{2,1,0:T(8,128)(2,1)S(1)} copy-done((bf16[1,64,256]{2,1,0:T(8,128)(2,1)S(1)}, bf16[1,64,256]{2,1,0:T(8,128)(2,1)}, u32[]{:S(2)}) %copy-start) | copy-done | bytes 32792
  0.8 0.0 copy-start.1
  0.8 0.7 %copy-done.1 = bf16[1,2,256]{2,1,0:T(2,128)(2,1)S(1)} copy-done((bf16[1,2,256]{2,1,0:T(2,128)(2,1)S(1)}, bf16[1,2,256]{2,1,0:T(2,128)(2,1)}, u32[]{:S(2)}) %copy-start.1) | copy-done | bytes 1048
  1.4 36.8 %als.1 = f32[1,64,256]{2,1,0:T(8,128)S(1)} custom-call(bf16[2,512,4096]{2,1,0:T(8,128)(2,1)} %x_hbm.1, bf16[1,64,256]{2,1,0:T(8,128)(2,1)S(1)} %copy-done, bf16[1,2,256]{2,1,0:T(2,128)(2,1)S(1)} %copy-done.1), custom_call_target="tpu_custom_call" | custom-call | flops 2147483648 | bytes 8388608 | tf_op jit(solution)/shard_map/als/pallas_call | solution.py:328
  38.3 0.6 %copy.5 = f32[1,64,256]{2,1,0:T(8,128)} copy(f32[1,64,256]{2,1,0:T(8,128)S(1)} %als.1) | data formatting | bytes 131072
Async XLA Ops:
  0.0 0.8 %copy-start = (bf16[1,64,256]{2,1,0:T(8,128)(2,1)S(1)}, bf16[1,64,256]{2,1,0:T(8,128)(2,1)}, u32[]{:S(2)}) copy-start(bf16[1,64,256]{2,1,0:T(8,128)(2,1)} %b_hbm.1) | copy-start | bytes 98308
  0.8 0.7 %copy-start.1 = (bf16[1,2,256]{2,1,0:T(2,128)(2,1)S(1)}, bf16[1,2,256]{2,1,0:T(2,128)(2,1)}, u32[]{:S(2)}) copy-start(bf16[1,2,256]{2,1,0:T(2,128)(2,1)} %c_ref.1) | copy-start | bytes 3076
